TPU v7x, 32 devices: a whole 2x2x4 slice. The times are simulated.
32 devices in a mesh: section: 8 (over z, y), rep: 4 (over x, core).
Axes of the slice: x: 2, y: 2, z: 4, core: 2. Of those that a mesh axis runs over, the one named last changes fastest.
Arguments:
- features: bfloat16 [4096, 256], P(('section', 'rep')), may hold values from -6 to 6
- tiles: bfloat16 [32, 64, 128, 128], P(('section', 'rep')), may hold values from 0 to 0.019042969
- columns: int32 [32, 64], P(('section', 'rep')), may hold values from 0 to 31
- weight: bfloat16 [256, 256], replicated, may hold values from -0.375 to 0.375
Outputs:
- hidden: bfloat16 [4096, 256], P(('section', 'rep'))
All inputs are finite; a program needn't handle non-finite values.
Results may differ from a plain program's by a relative error of at most 0.0049.
Values may be sent and summed in bfloat16 or wider, within the bound.
A program may use at most 64 MiB of HBM per device.

v0:
```python
import jax
import jax.numpy as jnp
from jax import lax
from jax.sharding import PartitionSpec as P


def on_device(features, tiles, columns, weight):
    width = features.shape[1]
    side = tiles.shape[2]
    group = lax.all_gather(features, "rep", axis=0, tiled=True)
    gathered = lax.all_gather(group, "section", axis=0, tiled=True)
    blocks = gathered.reshape(-1, side, width)
    picked = blocks[columns]
    summed = jnp.einsum("okij,okjf->oif", tiles, picked, preferred_element_type=jnp.float32)
    aggregated = summed.astype(jnp.bfloat16).reshape(-1, width)
    product = jnp.dot(aggregated, weight, preferred_element_type=jnp.float32)
    return jnp.maximum(product, 0.0).astype(jnp.bfloat16)


def solution(mesh):
    return jax.shard_map(
        on_device,
        mesh=mesh,
        in_specs=(
            P(("section", "rep"), None),
            P(("section", "rep"), None, None, None),
            P(("section", "rep"), None),
            P(),
        ),
        out_specs=P(("section", "rep"), None),
        check_vma=False,
    )
```

profile of v0, /device:TPU:0, one launch (start us, length us, event | category | flops | bytes accessed | tf_op | source)
XLA Modules:
  0.0 80.8 jit_solution(17621218261185126486)
XLA Ops:
  6.5 0.0 copy-start
  6.5 0.0 all-gather.2.cloned.1.call-start
  6.5 8.9 %all_gather.6 = bf16[512,256]{1,0:T(8,128)(2,1)} all-gather(bf16[128,256]{1,0:T(8,128)(2,1)} %param.4), channel_id=1, replica_groups=mesh['section'=8,'rep'=4] {'rep'}, dimensions={0}, use_global_device_ids=true | all-gather | bytes 327680 | tf_op jit(solution)/shard_map/all_gather | solution.py:10
  15.5 0.0 all-gather.2.cloned.1.call-update
  15.5 0.7 fusion.11
  16.2 49.1 %all-gather.2.cloned.1.call-done = bf16[4096,256]{1,0:T(8,128)(2,1)} async-done(((bf16[512,256]{1,0:T(8,128)(2,1)}), bf16[4096,256]{1,0:T(8,128)(2,1)}) %all-gather.2.cloned.1.call-update) | async-done | bytes 2097168 | tf_op jit(solution)/shard_map/all_gather | solution.py:11
  65.3 0.0 copy-start.1
  65.3 4.4 %gather_fusion = bf16[64,128,256]{2,1,0:T(8,128)(2,1)} fusion(bf16[32,128,256]{2,1,0:T(8,128)(2,1)} %bitcast.20, s32[1024]{0:T(1024)S(1)} %pad_clamp_fusion), kind=kCustom, calls=%fused_computation | custom fusion | bytes 8388864 | tf_op jit(solution)/shard_map/gather | solution.py:13
  69.7 0.0 copy-done
  69.7 0.0 copy-done.1
  69.7 4.3 %fusion.5 = bf16[128,256]{1,0:T(8,128)(2,1)} fusion(bf16[256,256]{1,0:T(8,128)(2,1)S(1)} %copy-done.1, bf16[64,128,256]{2,1,0:T(8,128)(2,1)} %gather_fusion, bf16[1,64,128,128]{3,2,1,0:T(8,128)(2,1)S(1)} %copy-done), kind=kOutput, calls=%fused_computation.5 | convolution fusion | flops 553746432 | bytes 6488064 | tf_op jit(solution)/shard_map/dot_general | solution.py:16
  (1 shorter events, 0.0 us)
Async XLA Ops:
  6.5 63.1 %copy-start = (bf16[1,64,128,128]{3,2,1,0:T(8,128)(2,1)S(1)}, bf16[1,64,128,128]{3,2,1,0:T(8,128)(2,1)}, u32[]{:S(2)}) copy-start(bf16[1,64,128,128]{3,2,1,0:T(8,128)(2,1)} %param.5) | copy-start | bytes 6291460
  6.5 58.8 %all-gather.2.cloned.1.call-start = ((), (), s32[]{:S(2)}) async-start(), calls=%async_computation | async-start | bytes 2359296 | tf_op jit(solution)/shard_map/all_gather | solution.py:11
  65.3 4.4 %copy-start.1 = (bf16[256,256]{1,0:T(8,128)(2,1)S(1)}, bf16[256,256]{1,0:T(8,128)(2,1)}, u32[]{:S(2)}) copy-start(bf16[256,256]{1,0:T(8,128)(2,1)} %param.7) | copy-start | bytes 393220
Sparse Core Ops, SparseCore 0:
  15.6 49.6 all-gather.1
where the time goes:
time: 81 us; the launch traced here: 80.8 us
  waiting for transfers between devices  49.1 us (61%)
  between operations  13.4 us (17%)
  blocking collectives  8.93 us (11%)
  local copies, waits for them, and re-layouts  4.38 us (5%)
  matrix products  4.29 us (5%)
    all_gather x1, waiting for transfers between devices, on_device(): gathered = lax.all_gather(group, 'section', axis=0, tiled=True)  49.1 us
    all_gather x1, blocking collectives, on_device(): group = lax.all_gather(features, 'rep', axis=0, tiled=True)  8.93 us
    gather x1, local copies, waits for them, and re-layouts, on_device(): picked = blocks[columns]  4.38 us
    dot_general x1, matrix products, on_device(): product = jnp.dot(aggregated, weight, preferred_element_type=jnp.float32)  4.29 us
  transfers between devices with their start and end apart: 1, of which 1 were waited for; matrix products, arithmetic and copies ran while one was open for 1% of the time, Pallas kernels for 0%

commit v1 on v0

v1 whole, which is shorter than its diff:
```python
import functools
import jax
import jax.numpy as jnp
from jax import lax
from jax.experimental import pallas as pl
from jax.experimental.pallas import tpu as pltpu
from jax.sharding import PartitionSpec as P

GROUP = 8


def flip(index, mask):
    bit = 1
    while bit <= mask:
        if mask & bit:
            index = index + bit - 2 * bit * ((index // bit) % 2)
        bit *= 2
    return index


def arrivals(columns, across):
    keys = []
    for m in range(columns):
        if m:
            keys.append(("column", m))
        keys.append(("beside", m))
        keys.append(("sibling", m, 0, 0))
        keys.append(("sibling", m, 1, 0))
        for q in range(1, across):
            keys.append(("across", m, q))
            keys.append(("diagonal", m, q, 0))
            keys.append(("diagonal", m, q, 1))
            keys.append(("sibling", m, 0, q))
            keys.append(("sibling diagonal", m, q, 0))
            keys.append(("sibling diagonal", m, q, 1))
    return {key: spot for spot, key in enumerate(keys)}


def kernel(columns, across, col_ref, f_ref, t_ref, w_ref, out_ref, blocks, tiles, weight, send_sems, recv_sems, local_sems):
    rep = 2 * across
    side = blocks.shape[1]
    half = side // 2
    section_at = lax.axis_index("section")
    rep_at = lax.axis_index("rep")
    a, b = section_at // 2, section_at % 2
    x, c = rep_at // 2, rep_at % 2
    spots = arrivals(columns, across)
    sent = []

    def device(m, beside, q, other):
        return flip(a, m) * 2 + flip(b, beside), flip(x, q) * 2 + flip(c, other)

    def block(m, beside, q, other=0):
        s, r = device(m, beside, q, other)
        return blocks.at[s * rep + r]

    def part(ref, h):
        return ref.at[pl.ds(h * half, half)]

    def send(src, dst, to, key):
        copy = pltpu.make_async_remote_copy(
            src_ref=src, dst_ref=dst, send_sem=send_sems.at[len(sent)], recv_sem=recv_sems.at[spots[key]],
            device_id=to, device_id_type=pl.DeviceIdType.MESH)
        copy.start()
        sent.append(copy)

    def arrive(dst, key):
        pltpu.make_async_remote_copy(
            src_ref=dst, dst_ref=dst, send_sem=send_sems.at[0], recv_sem=recv_sems.at[spots[key]],
            device_id=device(0, 0, 0, 1), device_id_type=pl.DeviceIdType.MESH).wait_recv()

    partners = [device(m, 0, 0, 0) for m in range(1, columns)]
    partners += [device(0, 0, q, 0) for q in range(1, across)]
    partners += [device(0, 1, 0, 0), device(0, 0, 0, 1)]
    barrier = pltpu.get_barrier_semaphore()
    for partner in partners:
        pl.semaphore_signal(barrier, inc=1, device_id=partner, device_id_type=pl.DeviceIdType.MESH)
    pl.semaphore_wait(barrier, len(partners))

    sibling = device(0, 0, 0, 1)
    beside = device(0, 1, 0, 0)

    def spread(src, m):
        for q in range(1, across):
            send(src, block(m, 0, 0), device(0, 0, q, 0), ("across", m, q))
        send(src, block(m, 0, 0), beside, ("beside", m))
        send(src, block(m, 0, 0), sibling, ("sibling", m, 0, 0))

    for m in range(1, columns):
        send(f_ref, block(0, 0, 0), device(m, 0, 0, 0), ("column", m))
    spread(f_ref, 0)
    own = pltpu.make_async_copy(f_ref, block(0, 0, 0), local_sems.at[0])
    load_tiles = pltpu.make_async_copy(t_ref, tiles, local_sems.at[1])
    load_weight = pltpu.make_async_copy(w_ref, weight, local_sems.at[2])
    own.start()
    load_tiles.start()
    load_weight.start()

    def relay(m):
        for q in range(1, across):
            got = block(m, 0, q)
            arrive(got, ("across", m, q))
            send(part(got, 0), part(got, 0), beside, ("diagonal", m, q, 0))
            send(got, got, sibling, ("sibling", m, 0, q))
        got = block(m, 1, 0)
        arrive(got, ("beside", m))
        for q in range(1, across):
            send(part(got, 1), part(got, 1), device(0, 0, q, 0), ("diagonal", m, q, 1))
        send(got, got, sibling, ("sibling", m, 1, 0))

    def diagonal(m):
        for q in range(1, across):
            for h in range(2):
                got = part(block(m, 1, q), h)
                arrive(got, ("diagonal", m, q, h))
                send(got, got, sibling, ("sibling diagonal", m, q, h))

    for m in range(1, columns):
        got = block(m, 0, 0)
        arrive(got, ("column", m))
        spread(got, m)
        relay(m - 1)
        if m > 1:
            diagonal(m - 2)
    relay(columns - 1)
    if columns > 1:
        diagonal(columns - 2)
    diagonal(columns - 1)

    for m in range(columns):
        arrive(block(m, 0, 0, 1), ("sibling", m, 0, 0))
        arrive(block(m, 1, 0, 1), ("sibling", m, 1, 0))
        for q in range(1, across):
            arrive(block(m, 0, q, 1), ("sibling", m, 0, q))
            for h in range(2):
                arrive(part(block(m, 1, q, 1), h), ("sibling diagonal", m, q, h))
    own.wait()
    load_tiles.wait()
    load_weight.wait()

    number = tiles.shape[1]
    group = GROUP if number % GROUP == 0 else 1

    def step(i, total):
        left = jnp.concatenate([tiles[0, i * group + g] for g in range(group)], axis=1)
        right = jnp.concatenate([blocks[col_ref[0, i * group + g]] for g in range(group)], axis=0)
        return total + jnp.dot(left, right, preferred_element_type=jnp.float32)

    total = lax.fori_loop(0, number // group, step, jnp.zeros(out_ref.shape, jnp.float32), unroll=True)
    aggregated = total.astype(jnp.bfloat16)
    product = jnp.dot(aggregated, weight[...], preferred_element_type=jnp.float32)
    out_ref[...] = jnp.maximum(product, 0.0).astype(out_ref.dtype)
    for copy in sent:
        copy.wait_send()


def on_device(sections, reps, features, tiles, columns, weight):
    along, across = sections // 2, reps // 2
    side, width = features.shape
    arriving = len(arrivals(along, across))
    return pl.pallas_call(
        functools.partial(kernel, along, across),
        out_shape=jax.ShapeDtypeStruct((side, weight.shape[1]), jnp.bfloat16),
        in_specs=[pl.BlockSpec(memory_space=pltpu.SMEM)] + [pl.BlockSpec(memory_space=pl.ANY)] * 3,
        out_specs=pl.BlockSpec(memory_space=pltpu.VMEM),
        scratch_shapes=[
            pltpu.VMEM((sections * reps, side, width), features.dtype),
            pltpu.VMEM(tiles.shape, tiles.dtype),
            pltpu.VMEM(weight.shape, weight.dtype),
            pltpu.SemaphoreType.DMA((arriving,)),
            pltpu.SemaphoreType.DMA((arriving,)),
            pltpu.SemaphoreType.DMA((3,)),
        ],
        compiler_params=pltpu.CompilerParams(
            collective_id=0, has_side_effects=True, vmem_limit_bytes=56 * 1024 * 1024),
        cost_estimate=pl.CostEstimate(
            flops=2 * tiles.size * width, bytes_accessed=2 * (tiles.size + features.size * sections * reps),
            transcendentals=0),
    )(columns, features, tiles, weight)


def solution(mesh):
    return jax.shard_map(
        functools.partial(on_device, mesh.shape["section"], mesh.shape["rep"]),
        mesh=mesh,
        in_specs=(
            P(("section", "rep"), None),
            P(("section", "rep"), None, None, None),
            P(("section", "rep"), None),
            P(),
        ),
        out_specs=P(("section", "rep"), None),
        check_vma=False,
    )
```

time: 81 us -> 25.4 us (0.31)
  the two profiles are of different devices: /device:TPU:0 before, /device:TPU:1 now
where the time goes in v1:
time: 25.4 us; the launch traced here: 25.3 us
  Pallas kernels  23.8 us (94%)
  local copies, waits for them, and re-layouts  1.47 us (6%)
    pallas_call x1, Pallas kernels, on_device(): pl.pallas_call(functools.partial(kernel, along, across), out_shape=jax.Sh...  23.8 us
    unnamed x1, local copies, waits for them, and re-layouts  1.47 us

profile of v1, /device:TPU:1, one launch (start us, length us, event | category | flops | bytes accessed | tf_op | source)
XLA Modules:
  0.0 25.3 jit_solution(8905004733638562419)
XLA Ops:
  0.0 23.8 %shard_map.46 = bf16[128,256]{1,0:T(8,128)(2,1)} custom-call(s32[1,64]{1,0:T(1,128)} %col_ref.1, bf16[128,256]{1,0:T(8,128)(2,1)} %f_ref.1, bf16[1,64,128,128]{3,2,1,0:T(8,128)(2,1)} %t_ref.1, bf16[256,256]{1,0:T(8,128)(2,1)} %w_ref.1), custom_call_target="tpu_custom_call" | custom-call | flops 536870912 | bytes 4194304 | tf_op jit(solution)/shard_map/pallas_call | solution.py:161
  23.8 1.5 %copy.6 = bf16[128,256]{1,0:T(8,128)(2,1)} copy(bf16[128,256]{1,0:T(8,128)(2,1)} %shard_map.46) | data formatting | bytes 131072

commit v2 on v0

v2 whole, which is shorter than its diff:
```python
import functools
import jax
import jax.numpy as jnp
from jax import lax
from jax.experimental import pallas as pl
from jax.experimental.pallas import tpu as pltpu
from jax.sharding import PartitionSpec as P

GROUP = 8

def flip(index, wanted):
    return index + wanted - 2 * wanted * (index % 2)

def steps_of(columns):
    return [(0, 0)] + [(side, s) for s in range(1, columns) for side in (-1, 1)]

def arrivals(columns, across):
    keys = []
    for item in steps_of(columns):
        if item[1]:
            keys.append(("column", item))
        keys.append(("beside", item))
        keys.append(("sibling", item, 0, 0))
        keys.append(("sibling", item, 1, 0))
        for q in range(1, across):
            keys.append(("across", item, q))
            keys.append(("diagonal", item, q, 0))
            keys.append(("diagonal", item, q, 1))
            keys.append(("sibling", item, 0, q))
            keys.append(("sibling diagonal", item, q, 0))
            keys.append(("sibling diagonal", item, q, 1))
    return {key: spot for spot, key in enumerate(keys)}

def kernel(columns, across, col_ref, f_ref, t_ref, w_ref, out_ref, blocks, tiles, weight, send_sems, recv_sems, local_sems):
    rep = 2 * across
    side_rows = blocks.shape[1]
    half = side_rows // 2
    section_at = lax.axis_index("section")
    rep_at = lax.axis_index("rep")
    a, b = section_at // 2, section_at % 2
    x, c = rep_at // 2, rep_at % 2
    spots = arrivals(columns, across)
    sent = []

    def device(item, beside, q, other):
        at = lax.rem(x + q, across) if q else x
        return (a + item[0] * item[1]) * 2 + flip(b, beside), at * 2 + flip(c, other)

    here = (0, 0)

    def block(item, beside, q, other=0):
        s, r = device(item, beside, q, other)
        return blocks.at[s * rep + r]

    def part(ref, h):
        return ref.at[pl.ds(h * half, half)]

    def there(item):
        if item[1] == 0:
            return None
        return a >= item[1] if item[0] < 0 else a + item[1] < columns

    def both(item, condition):
        known = there(item)
        return condition if known is None else known & condition

    def only(condition, work):
        if condition is None:
            work()
        else:
            pl.when(condition)(work)

    def send(src, dst, to, key, condition):
        copy = pltpu.make_async_remote_copy(
            src_ref=src, dst_ref=dst, send_sem=send_sems.at[spots[key]], recv_sem=recv_sems.at[spots[key]],
            device_id=to, device_id_type=pl.DeviceIdType.MESH)
        copy.start()
        sent.append((src.shape[0], key, condition))

    def arrive(dst, key):
        pltpu.make_async_remote_copy(
            src_ref=dst, dst_ref=dst, send_sem=send_sems.at[0], recv_sem=recv_sems.at[spots[key]],
            device_id=device(here, 0, 0, 1), device_id_type=pl.DeviceIdType.MESH).wait_recv()

    below, above = device((-1, 1), 0, 0, 0), device((1, 1), 0, 0, 0)
    has_below, has_above = a >= 1, a + 1 < columns
    sibling = device(here, 0, 0, 1)
    beside = device(here, 1, 0, 0)

    barrier = pltpu.get_barrier_semaphore()

    def greet(partner):
        pl.semaphore_signal(barrier, inc=1, device_id=partner, device_id_type=pl.DeviceIdType.MESH)

    partners = [device(here, 0, q, 0) for q in range(1, across)] + [beside, sibling]
    for partner in partners:
        greet(partner)
    only(has_below, lambda: greet(below))
    only(has_above, lambda: greet(above))
    pl.semaphore_wait(barrier, len(partners) + jnp.where(has_below, 1, 0) + jnp.where(has_above, 1, 0))

    def pass_on(src, item):
        s = item[1] + 1
        dst = block(item, 0, 0)
        if item[0] <= 0 and s < columns:
            only(has_above, lambda: send(src, dst, above, ("column", (-1, s)), lambda: both(item, has_above)))
        if item[0] >= 0 and s < columns:
            only(has_below, lambda: send(src, dst, below, ("column", (1, s)), lambda: both(item, has_below)))

    def spread(src, item):
        dst = block(item, 0, 0)
        for q in range(1, across):
            send(src, dst, device(here, 0, q, 0), ("across", item, q), lambda: there(item))
        send(src, dst, beside, ("beside", item), lambda: there(item))
        send(src, dst, sibling, ("sibling", item, 0, 0), lambda: there(item))

    def receive(item):
        got = block(item, 0, 0)
        arrive(got, ("column", item))
        pass_on(got, item)
        spread(got, item)

    def relay(item):
        for q in range(1, across):
            got = block(item, 0, across - q)
            arrive(got, ("across", item, q))
            send(part(got, 0), part(got, 0), beside, ("diagonal", item, q, 0), lambda: there(item))
            send(got, got, sibling, ("sibling", item, 0, q), lambda: there(item))
        got = block(item, 1, 0)
        arrive(got, ("beside", item))
        for q in range(1, across):
            send(part(got, 1), part(got, 1), device(here, 0, q, 0), ("diagonal", item, q, 1), lambda: there(item))
        send(got, got, sibling, ("sibling", item, 1, 0), lambda: there(item))

    def diagonal(item):
        for q in range(1, across):
            for h in range(2):
                got = part(block(item, 1, across - q), h)
                arrive(got, ("diagonal", item, q, h))
                send(got, got, sibling, ("sibling diagonal", item, q, h), lambda: there(item))

    def from_sibling(item):
        arrive(block(item, 0, 0, 1), ("sibling", item, 0, 0))
        arrive(block(item, 1, 0, 1), ("sibling", item, 1, 0))
        for q in range(1, across):
            arrive(block(item, 0, across - q, 1), ("sibling", item, 0, q))
            for h in range(2):
                arrive(part(block(item, 1, across - q, 1), h), ("sibling diagonal", item, q, h))

    pass_on(f_ref, here)
    spread(f_ref, here)
    own = pltpu.make_async_copy(f_ref, block(here, 0, 0), local_sems.at[0])
    load_tiles = pltpu.make_async_copy(t_ref, tiles, local_sems.at[1])
    load_weight = pltpu.make_async_copy(w_ref, weight, local_sems.at[2])
    own.start()
    load_tiles.start()
    load_weight.start()

    rounds = [[here]] + [[(-1, s), (1, s)] for s in range(1, columns)]
    for s in range(len(rounds) + 2):
        for stage, at in ((receive, s), (relay, s - 1), (diagonal, s - 2)):
            if 0 <= at < len(rounds) and not (stage is receive and at == 0):
                for item in rounds[at]:
                    only(there(item), functools.partial(stage, item))
    for items in rounds:
        for item in items:
            only(there(item), functools.partial(from_sibling, item))
    own.wait()
    load_tiles.wait()
    load_weight.wait()

    number = tiles.shape[1]
    group = GROUP if number % GROUP == 0 else 1

    def step(i, total):
        left = jnp.concatenate([tiles[0, i * group + g] for g in range(group)], axis=1)
        right = jnp.concatenate([blocks[col_ref[0, i * group + g]] for g in range(group)], axis=0)
        return total + jnp.dot(left, right, preferred_element_type=jnp.float32)

    total = lax.fori_loop(0, number // group, step, jnp.zeros(out_ref.shape, jnp.float32), unroll=True)
    aggregated = total.astype(jnp.bfloat16)
    product = jnp.dot(aggregated, weight[...], preferred_element_type=jnp.float32)
    out_ref[...] = jnp.maximum(product, 0.0).astype(out_ref.dtype)

    def gone(rows, key):
        src = blocks.at[0, pl.ds(0, rows)]
        pltpu.make_async_remote_copy(
            src_ref=src, dst_ref=src, send_sem=send_sems.at[spots[key]], recv_sem=recv_sems.at[spots[key]],
            device_id=sibling, device_id_type=pl.DeviceIdType.MESH).wait_send()

    for rows, key, condition in sent:
        only(condition(), functools.partial(gone, rows, key))

def on_device(sections, reps, features, tiles, columns, weight):
    along, across = sections // 2, reps // 2
    side, width = features.shape
    arriving = len(arrivals(along, across))

    return pl.pallas_call(
        functools.partial(kernel, along, across),
        out_shape=jax.ShapeDtypeStruct((side, weight.shape[1]), jnp.bfloat16),
        in_specs=[pl.BlockSpec(memory_space=pltpu.SMEM)] + [pl.BlockSpec(memory_space=pltpu.HBM)] * 3,
        out_specs=pl.BlockSpec(memory_space=pltpu.VMEM),
        scratch_shapes=[
            pltpu.VMEM((sections * reps, side, width), features.dtype),
            pltpu.VMEM(tiles.shape, tiles.dtype),
            pltpu.VMEM(weight.shape, weight.dtype),
            pltpu.SemaphoreType.DMA((arriving,)),
            pltpu.SemaphoreType.DMA((arriving,)),
            pltpu.SemaphoreType.DMA((3,)),
        ],
        compiler_params=pltpu.CompilerParams(
            collective_id=0, has_side_effects=True, vmem_limit_bytes=56 * 1024 * 1024),
        cost_estimate=pl.CostEstimate(
            flops=2 * tiles.size * width, bytes_accessed=2 * (tiles.size + features.size * sections * reps),
            transcendentals=0),
    )(columns, features, tiles, weight)

def solution(mesh):
    return jax.shard_map(
        functools.partial(on_device, mesh.shape["section"], mesh.shape["rep"]),
        mesh=mesh,
        in_specs=(
            P(("section", "rep"), None),
            P(("section", "rep"), None, None, None),
            P(("section", "rep"), None),
            P(),
        ),
        out_specs=P(("section", "rep"), None),
        check_vma=False,
    )
```

time: 81 us -> 27.1 us (0.33)
  the two profiles are of different devices: /device:TPU:0 before, /device:TPU:1 now
where the time goes in v2:
time: 27.1 us; the launch traced here: 26.9 us
  Pallas kernels  25.4 us (94%)
  local copies, waits for them, and re-layouts  1.47 us (5%)
    pallas_call x1, Pallas kernels, on_device(): pl.pallas_call(functools.partial(kernel, along, across), out_shape=jax.Sh...  25.4 us
    unnamed x1, local copies, waits for them, and re-layouts  1.47 us

profile of v2, /device:TPU:1, one launch (start us, length us, event | category | flops | bytes accessed | tf_op | source)
XLA Modules:
  0.0 26.9 jit_solution(11060475595319970772)
XLA Ops:
  0.0 25.4 %shard_map.46 = bf16[128,256]{1,0:T(8,128)(2,1)} custom-call(s32[1,64]{1,0:T(1,128)} %col_ref.1, bf16[128,256]{1,0:T(8,128)(2,1)} %f_ref.1, bf16[1,64,128,128]{3,2,1,0:T(8,128)(2,1)} %t_ref.1, bf16[256,256]{1,0:T(8,128)(2,1)} %w_ref.1), custom_call_target="tpu_custom_call" | custom-call | flops 536870912 | bytes 4194304 | tf_op jit(solution)/shard_map/pallas_call | solution.py:199
  25.5 1.5 %copy.6 = bf16[128,256]{1,0:T(8,128)(2,1)} copy(bf16[128,256]{1,0:T(8,128)(2,1)} %shard_map.46) | data formatting | bytes 131072

commit v3 on v1

--- a/solution.py
+++ b/solution.py
@@ -81,14 +81,20 @@
     beside = device(0, 1, 0, 0)
 
     def spread(src, m):
-        for q in range(1, across):
-            send(src, block(m, 0, 0), device(0, 0, q, 0), ("across", m, q))
-        send(src, block(m, 0, 0), beside, ("beside", m))
+        if m != 1:
+            for q in range(1, across):
+                send(src, block(m, 0, 0), device(0, 0, q, 0), ("across", m, q))
+            send(src, block(m, 0, 0), beside, ("beside", m))
         send(src, block(m, 0, 0), sibling, ("sibling", m, 0, 0))
 
-    for m in range(1, columns):
+    def climb(m):
         send(f_ref, block(0, 0, 0), device(m, 0, 0, 0), ("column", m))
+
+    for m in range(2, columns):
+        climb(m)
     spread(f_ref, 0)
+    if columns > 1:
+        climb(1)
     own = pltpu.make_async_copy(f_ref, block(0, 0, 0), local_sems.at[0])
     load_tiles = pltpu.make_async_copy(t_ref, tiles, local_sems.at[1])
     load_weight = pltpu.make_async_copy(w_ref, weight, local_sems.at[2])
@@ -101,11 +107,15 @@
             got = block(m, 0, q)
             arrive(got, ("across", m, q))
             send(part(got, 0), part(got, 0), beside, ("diagonal", m, q, 0))
+            if m == 0 and columns > 1:
+                send(got, got, device(1, 0, 0, 0), ("across", 1, q))
             send(got, got, sibling, ("sibling", m, 0, q))
         got = block(m, 1, 0)
         arrive(got, ("beside", m))
         for q in range(1, across):
             send(part(got, 1), part(got, 1), device(0, 0, q, 0), ("diagonal", m, q, 1))
+        if m == 0 and columns > 1:
+            send(got, got, device(1, 0, 0, 0), ("beside", 1))
         send(got, got, sibling, ("sibling", m, 1, 0))
 
     def diagonal(m):
@@ -115,17 +125,29 @@
                 arrive(got, ("diagonal", m, q, h))
                 send(got, got, sibling, ("sibling diagonal", m, q, h))
 
-    for m in range(1, columns):
+    def column(m):
         got = block(m, 0, 0)
         arrive(got, ("column", m))
         spread(got, m)
+
+    relay(0)
+    late = list(range(2, columns))
+    for m in late[:1]:
+        column(m)
+    diagonal(0)
+    if columns > 1:
+        column(1)
+        relay(1)
+    for m in late[1:]:
+        column(m)
         relay(m - 1)
-        if m > 1:
-            diagonal(m - 2)
-    relay(columns - 1)
     if columns > 1:
-        diagonal(columns - 2)
-    diagonal(columns - 1)
+        diagonal(1)
+    for m in late[:-1]:
+        diagonal(m)
+    for m in late[-1:]:
+        relay(m)
+        diagonal(m)
 
     for m in range(columns):
         arrive(block(m, 0, 0, 1), ("sibling", m, 0, 0))

time: 25.4 us -> 27 us (1.063)
  Pallas kernels: 23.8 us -> 25.4 us
    pallas_call x1, Pallas kernels: 23.8 us -> 25.4 us  [on_device(): pl.pallas_call(functools.partial(kernel, along, across), out_shape=jax.Sh...]
where the time goes in v3:
time: 27 us; the launch traced here: 26.8 us
  Pallas kernels  25.4 us (94%)
  local copies, waits for them, and re-layouts  1.47 us (5%)
    pallas_call x1, Pallas kernels, on_device(): pl.pallas_call(functools.partial(kernel, along, across), out_shape=jax.Sh...  25.4 us
    unnamed x1, local copies, waits for them, and re-layouts  1.47 us

profile of v3, /device:TPU:1, one launch (start us, length us, event | category | flops | bytes accessed | tf_op | source)
XLA Modules:
  0.0 26.8 jit_solution(5790072206843727131)
XLA Ops:
  0.0 25.4 %shard_map.46 = bf16[128,256]{1,0:T(8,128)(2,1)} custom-call(s32[1,64]{1,0:T(1,128)} %col_ref.1, bf16[128,256]{1,0:T(8,128)(2,1)} %f_ref.1, bf16[1,64,128,128]{3,2,1,0:T(8,128)(2,1)} %t_ref.1, bf16[256,256]{1,0:T(8,128)(2,1)} %w_ref.1), custom_call_target="tpu_custom_call" | custom-call | flops 536870912 | bytes 4194304 | tf_op jit(solution)/shard_map/pallas_call | solution.py:183
  25.4 1.5 %copy.6 = bf16[128,256]{1,0:T(8,128)(2,1)} copy(bf16[128,256]{1,0:T(8,128)(2,1)} %shard_map.46) | data formatting | bytes 131072

commit v4 on v2

--- a/solution.py
+++ b/solution.py
@@ -24,11 +24,9 @@
         keys.append(("sibling", item, 1, 0))
         for q in range(1, across):
             keys.append(("across", item, q))
-            keys.append(("diagonal", item, q, 0))
-            keys.append(("diagonal", item, q, 1))
+            keys.extend(("diagonal", item, q, h) for h in range(3))
             keys.append(("sibling", item, 0, q))
-            keys.append(("sibling diagonal", item, q, 0))
-            keys.append(("sibling diagonal", item, q, 1))
+            keys.extend(("sibling diagonal", item, q, h) for h in range(3))
     return {key: spot for spot, key in enumerate(keys)}
 
 def kernel(columns, across, col_ref, f_ref, t_ref, w_ref, out_ref, blocks, tiles, weight, send_sems, recv_sems, local_sems):
@@ -40,7 +38,7 @@
     a, b = section_at // 2, section_at % 2
     x, c = rep_at // 2, rep_at % 2
     spots = arrivals(columns, across)
-    sent = []
+    sent, climbed = [], []
 
     def device(item, beside, q, other):
         at = lax.rem(x + q, across) if q else x
@@ -52,17 +50,22 @@
         s, r = device(item, beside, q, other)
         return blocks.at[s * rep + r]
 
+    def direct(item):
+        return item[1] in (0, columns - 1)
+
+    def pieces(item):
+        return (0,) if direct(item) else (1, 2)
+
     def part(ref, h):
+        if h == 0:
+            return ref
+        h = h - 1
         return ref.at[pl.ds(h * half, half)]
 
     def there(item):
         if item[1] == 0:
             return None
         return a >= item[1] if item[0] < 0 else a + item[1] < columns
-
-    def both(item, condition):
-        known = there(item)
-        return condition if known is None else known & condition
 
     def only(condition, work):
         if condition is None:
@@ -75,15 +78,20 @@
             src_ref=src, dst_ref=dst, send_sem=send_sems.at[spots[key]], recv_sem=recv_sems.at[spots[key]],
             device_id=to, device_id_type=pl.DeviceIdType.MESH)
         copy.start()
-        sent.append((src.shape[0], key, condition))
+        if condition is not None:
+            sent.append((src.shape[0], key, condition))
 
     def arrive(dst, key):
         pltpu.make_async_remote_copy(
             src_ref=dst, dst_ref=dst, send_sem=send_sems.at[0], recv_sem=recv_sems.at[spots[key]],
             device_id=device(here, 0, 0, 1), device_id_type=pl.DeviceIdType.MESH).wait_recv()
 
-    below, above = device((-1, 1), 0, 0, 0), device((1, 1), 0, 0, 0)
-    has_below, has_above = a >= 1, a + 1 < columns
+    def gone(rows, key):
+        src = blocks.at[0, pl.ds(0, rows)]
+        pltpu.make_async_remote_copy(
+            src_ref=src, dst_ref=src, send_sem=send_sems.at[spots[key]], recv_sem=recv_sems.at[spots[key]],
+            device_id=device(here, 0, 0, 1), device_id_type=pl.DeviceIdType.MESH).wait_send()
+
     sibling = device(here, 0, 0, 1)
     beside = device(here, 1, 0, 0)
 
@@ -93,48 +101,55 @@
         pl.semaphore_signal(barrier, inc=1, device_id=partner, device_id_type=pl.DeviceIdType.MESH)
 
     partners = [device(here, 0, q, 0) for q in range(1, across)] + [beside, sibling]
+    partners += [device(here, 1, q, 0) for q in range(1, across)]
+    partners += [(lax.rem(a + d, columns) * 2 + b, rep_at) for d in range(1, columns)]
     for partner in partners:
         greet(partner)
-    only(has_below, lambda: greet(below))
-    only(has_above, lambda: greet(above))
-    pl.semaphore_wait(barrier, len(partners) + jnp.where(has_below, 1, 0) + jnp.where(has_above, 1, 0))
-
-    def pass_on(src, item):
-        s = item[1] + 1
-        dst = block(item, 0, 0)
-        if item[0] <= 0 and s < columns:
-            only(has_above, lambda: send(src, dst, above, ("column", (-1, s)), lambda: both(item, has_above)))
-        if item[0] >= 0 and s < columns:
-            only(has_below, lambda: send(src, dst, below, ("column", (1, s)), lambda: both(item, has_below)))
+    pl.semaphore_wait(barrier, len(partners))
+
+    def climb(s):
+        for side, condition in ((-1, a + s < columns), (1, a >= s)):
+            to, key = device((-side, s), 0, 0, 0), ("column", (side, s))
+            only(condition, functools.partial(send, f_ref, block(here, 0, 0), to, key, None))
+            climbed.append((s, key, condition))
+
+    def wait_climb(s):
+        for distance, key, condition in climbed:
+            if distance == s:
+                only(condition, functools.partial(gone, f_ref.shape[0], key))
 
     def spread(src, item):
         dst = block(item, 0, 0)
         for q in range(1, across):
             send(src, dst, device(here, 0, q, 0), ("across", item, q), lambda: there(item))
         send(src, dst, beside, ("beside", item), lambda: there(item))
+        if direct(item):
+            for q in range(1, across):
+                send(src, dst, device(here, 1, q, 0), ("diagonal", item, q, 0), lambda: there(item))
         send(src, dst, sibling, ("sibling", item, 0, 0), lambda: there(item))
 
     def receive(item):
         got = block(item, 0, 0)
         arrive(got, ("column", item))
-        pass_on(got, item)
         spread(got, item)
 
     def relay(item):
         for q in range(1, across):
             got = block(item, 0, across - q)
             arrive(got, ("across", item, q))
-            send(part(got, 0), part(got, 0), beside, ("diagonal", item, q, 0), lambda: there(item))
+            if not direct(item):
+                send(part(got, 1), part(got, 1), beside, ("diagonal", item, q, 1), lambda: there(item))
             send(got, got, sibling, ("sibling", item, 0, q), lambda: there(item))
         got = block(item, 1, 0)
         arrive(got, ("beside", item))
         for q in range(1, across):
-            send(part(got, 1), part(got, 1), device(here, 0, q, 0), ("diagonal", item, q, 1), lambda: there(item))
+            if not direct(item):
+                send(part(got, 2), part(got, 2), device(here, 0, q, 0), ("diagonal", item, q, 2), lambda: there(item))
         send(got, got, sibling, ("sibling", item, 1, 0), lambda: there(item))
 
     def diagonal(item):
         for q in range(1, across):
-            for h in range(2):
+            for h in pieces(item):
                 got = part(block(item, 1, across - q), h)
                 arrive(got, ("diagonal", item, q, h))
                 send(got, got, sibling, ("sibling diagonal", item, q, h), lambda: there(item))
@@ -144,10 +159,11 @@
         arrive(block(item, 1, 0, 1), ("sibling", item, 1, 0))
         for q in range(1, across):
             arrive(block(item, 0, across - q, 1), ("sibling", item, 0, q))
-            for h in range(2):
+            for h in pieces(item):
                 arrive(part(block(item, 1, across - q, 1), h), ("sibling diagonal", item, q, h))
 
-    pass_on(f_ref, here)
+    if columns > 1:
+        climb(1)
     spread(f_ref, here)
     own = pltpu.make_async_copy(f_ref, block(here, 0, 0), local_sems.at[0])
     load_tiles = pltpu.make_async_copy(t_ref, tiles, local_sems.at[1])
@@ -158,6 +174,9 @@
 
     rounds = [[here]] + [[(-1, s), (1, s)] for s in range(1, columns)]
     for s in range(len(rounds) + 2):
+        if s + 1 < columns and s > 0:
+            wait_climb(s)
+            climb(s + 1)
         for stage, at in ((receive, s), (relay, s - 1), (diagonal, s - 2)):
             if 0 <= at < len(rounds) and not (stage is receive and at == 0):
                 for item in rounds[at]:
@@ -182,20 +201,16 @@
     product = jnp.dot(aggregated, weight[...], preferred_element_type=jnp.float32)
     out_ref[...] = jnp.maximum(product, 0.0).astype(out_ref.dtype)
 
-    def gone(rows, key):
-        src = blocks.at[0, pl.ds(0, rows)]
-        pltpu.make_async_remote_copy(
-            src_ref=src, dst_ref=src, send_sem=send_sems.at[spots[key]], recv_sem=recv_sems.at[spots[key]],
-            device_id=sibling, device_id_type=pl.DeviceIdType.MESH).wait_send()
-
+    if columns > 1:
+        wait_climb(columns - 1)
     for rows, key, condition in sent:
         only(condition(), functools.partial(gone, rows, key))
+
 
 def on_device(sections, reps, features, tiles, columns, weight):
     along, across = sections // 2, reps // 2
     side, width = features.shape
     arriving = len(arrivals(along, across))
-
     return pl.pallas_call(
         functools.partial(kernel, along, across),
         out_shape=jax.ShapeDtypeStruct((side, weight.shape[1]), jnp.bfloat16),

time: 27.1 us -> 25.8 us (0.952)
  Pallas kernels: 25.4 us -> 24.1 us
    pallas_call x1, Pallas kernels: 25.4 us -> 24.1 us  [on_device(): pl.pallas_call(functools.partial(kernel, along, across), out_shape=jax.Sh...]
where the time goes in v4:
time: 25.8 us; the launch traced here: 25.6 us
  Pallas kernels  24.1 us (93%)
  local copies, waits for them, and re-layouts  1.47 us (6%)
    pallas_call x1, Pallas kernels, on_device(): pl.pallas_call(functools.partial(kernel, along, across), out_shape=jax.Sh...  24.1 us
    unnamed x1, local copies, waits for them, and re-layouts  1.47 us

profile of v4, /device:TPU:1, one launch (start us, length us, event | category | flops | bytes accessed | tf_op | source)
XLA Modules:
  0.0 25.6 jit_solution(10876500545021136155)
XLA Ops:
  0.0 24.1 %shard_map.46 = bf16[128,256]{1,0:T(8,128)(2,1)} custom-call(s32[1,64]{1,0:T(1,128)} %col_ref.1, bf16[128,256]{1,0:T(8,128)(2,1)} %f_ref.1, bf16[1,64,128,128]{3,2,1,0:T(8,128)(2,1)} %t_ref.1, bf16[256,256]{1,0:T(8,128)(2,1)} %w_ref.1), custom_call_target="tpu_custom_call" | custom-call | flops 536870912 | bytes 4194304 | tf_op jit(solution)/shard_map/pallas_call | solution.py:214
  24.1 1.5 %copy.6 = bf16[128,256]{1,0:T(8,128)(2,1)} copy(bf16[128,256]{1,0:T(8,128)(2,1)} %shard_map.46) | data formatting | bytes 131072

commit v5 on v4

--- a/solution.py
+++ b/solution.py
@@ -29,7 +29,7 @@
             keys.extend(("sibling diagonal", item, q, h) for h in range(3))
     return {key: spot for spot, key in enumerate(keys)}
 
-def kernel(columns, across, col_ref, f_ref, t_ref, w_ref, out_ref, blocks, tiles, weight, send_sems, recv_sems, local_sems):
+def kernel(columns, across, c_ref, f_ref, t_ref, w_ref, out_ref, blocks, tiles, weight, col_ref, send_sems, recv_sems, local_sems):
     rep = 2 * across
     side_rows = blocks.shape[1]
     half = side_rows // 2
@@ -168,7 +168,9 @@
     own = pltpu.make_async_copy(f_ref, block(here, 0, 0), local_sems.at[0])
     load_tiles = pltpu.make_async_copy(t_ref, tiles, local_sems.at[1])
     load_weight = pltpu.make_async_copy(w_ref, weight, local_sems.at[2])
+    load_columns = pltpu.make_async_copy(c_ref, col_ref, local_sems.at[3])
     own.start()
+    load_columns.start()
     load_tiles.start()
     load_weight.start()
 
@@ -185,6 +187,7 @@
         for item in items:
             only(there(item), functools.partial(from_sibling, item))
     own.wait()
+    load_columns.wait()
     load_tiles.wait()
     load_weight.wait()
 
@@ -196,7 +199,7 @@
         right = jnp.concatenate([blocks[col_ref[0, i * group + g]] for g in range(group)], axis=0)
         return total + jnp.dot(left, right, preferred_element_type=jnp.float32)
 
-    total = lax.fori_loop(0, number // group, step, jnp.zeros(out_ref.shape, jnp.float32), unroll=True)
+    total = lax.fori_loop(0, number // group, step, jnp.zeros(out_ref.shape, jnp.float32))
     aggregated = total.astype(jnp.bfloat16)
     product = jnp.dot(aggregated, weight[...], preferred_element_type=jnp.float32)
     out_ref[...] = jnp.maximum(product, 0.0).astype(out_ref.dtype)
@@ -213,16 +216,17 @@
     arriving = len(arrivals(along, across))
     return pl.pallas_call(
         functools.partial(kernel, along, across),
-        out_shape=jax.ShapeDtypeStruct((side, weight.shape[1]), jnp.bfloat16),
-        in_specs=[pl.BlockSpec(memory_space=pltpu.SMEM)] + [pl.BlockSpec(memory_space=pltpu.HBM)] * 3,
+        out_shape=pltpu.VMEM((side, weight.shape[1]), jnp.bfloat16),
+        in_specs=[pl.BlockSpec(memory_space=pltpu.HBM)] * 4,
         out_specs=pl.BlockSpec(memory_space=pltpu.VMEM),
         scratch_shapes=[
             pltpu.VMEM((sections * reps, side, width), features.dtype),
             pltpu.VMEM(tiles.shape, tiles.dtype),
             pltpu.VMEM(weight.shape, weight.dtype),
+            pltpu.SMEM(columns.shape, columns.dtype),
             pltpu.SemaphoreType.DMA((arriving,)),
             pltpu.SemaphoreType.DMA((arriving,)),
-            pltpu.SemaphoreType.DMA((3,)),
+            pltpu.SemaphoreType.DMA((4,)),
         ],
         compiler_params=pltpu.CompilerParams(
             collective_id=0, has_side_effects=True, vmem_limit_bytes=56 * 1024 * 1024),

time: 25.8 us -> 24.8 us (0.961)
  local copies, waits for them, and re-layouts: 1.47 us -> 0.63 us
    unnamed x1, local copies, waits for them, and re-layouts: 1.47 us -> 0.63 us
where the time goes in v5:
time: 24.8 us; the launch traced here: 24.7 us
  Pallas kernels  24 us (97%)
  local copies, waits for them, and re-layouts  0.63 us (3%)
    pallas_call x1, Pallas kernels, on_device(): pl.pallas_call(functools.partial(kernel, along, across), out_shape=pltpu....  24 us
    unnamed x1, local copies, waits for them, and re-layouts  0.63 us

profile of v5, /device:TPU:1, one launch (start us, length us, event | category | flops | bytes accessed | tf_op | source)
XLA Modules:
  0.0 24.7 jit_solution(2325322361760704675)
XLA Ops:
  0.0 24.0 %shard_map.46 = bf16[128,256]{1,0:T(8,128)(2,1)S(1)} custom-call(s32[1,64]{1,0:T(1,128)} %c_ref.1, bf16[128,256]{1,0:T(8,128)(2,1)} %f_ref.1, bf16[1,64,128,128]{3,2,1,0:T(8,128)(2,1)} %t_ref.1, bf16[256,256]{1,0:T(8,128)(2,1)} %w_ref.1), custom_call_target="tpu_custom_call" | custom-call | flops 536870912 | bytes 4194304 | tf_op jit(solution)/shard_map/pallas_call | solution.py:217
  24.0 0.6 %copy.6 = bf16[128,256]{1,0:T(8,128)(2,1)} copy(bf16[128,256]{1,0:T(8,128)(2,1)S(1)} %shard_map.46) | data formatting | bytes 131072

commit v6 on v5

--- a/solution.py
+++ b/solution.py
@@ -51,7 +51,7 @@
         return blocks.at[s * rep + r]
 
     def direct(item):
-        return item[1] in (0, columns - 1)
+        return item[1] > 1 and item[1] == columns - 1
 
     def pieces(item):
         return (0,) if direct(item) else (1, 2)
@@ -118,6 +118,11 @@
             if distance == s:
                 only(condition, functools.partial(gone, f_ref.shape[0], key))
 
+    def pass_on(src, item):
+        on = a + 1 < columns if item[0] < 0 else a >= 1
+        to, key = device((-item[0], 1), 0, 0, 0), ("column", (item[0], 2))
+        only(on, lambda: send(src, src, to, key, None))
+
     def spread(src, item):
         dst = block(item, 0, 0)
         for q in range(1, across):
@@ -131,6 +136,8 @@
     def receive(item):
         got = block(item, 0, 0)
         arrive(got, ("column", item))
+        if item[1] == 1 and columns > 2:
+            pass_on(got, item)
         spread(got, item)
 
     def relay(item):
@@ -174,11 +181,12 @@
     load_tiles.start()
     load_weight.start()
 
+    for s in range(3, columns):
+        wait_climb(1 if s == 3 else s - 1)
+        climb(s)
+
     rounds = [[here]] + [[(-1, s), (1, s)] for s in range(1, columns)]
     for s in range(len(rounds) + 2):
-        if s + 1 < columns and s > 0:
-            wait_climb(s)
-            climb(s + 1)
         for stage, at in ((receive, s), (relay, s - 1), (diagonal, s - 2)):
             if 0 <= at < len(rounds) and not (stage is receive and at == 0):
                 for item in rounds[at]:
@@ -205,7 +213,10 @@
     out_ref[...] = jnp.maximum(product, 0.0).astype(out_ref.dtype)
 
     if columns > 1:
-        wait_climb(columns - 1)
+        wait_climb(columns - 1 if columns > 3 else 1)
+    if columns > 2:
+        for item, condition in (((-1, 2), (a >= 1) & (a + 1 < columns)), ((1, 2), (a >= 1) & (a + 1 < columns))):
+            only(condition, functools.partial(gone, f_ref.shape[0], ("column", item)))
     for rows, key, condition in sent:
         only(condition(), functools.partial(gone, rows, key))
 

time: 24.8 us -> 25.5 us (1.028)
  Pallas kernels: 24 us -> 24.7 us
    pallas_call x1, Pallas kernels: 24 us -> 24.7 us  [on_device(): pl.pallas_call(functools.partial(kernel, along, across), out_shape=pltpu....]
where the time goes in v6:
time: 25.5 us; the launch traced here: 25.3 us
  Pallas kernels  24.7 us (97%)
  local copies, waits for them, and re-layouts  0.63 us (2%)
    pallas_call x1, Pallas kernels, on_device(): pl.pallas_call(functools.partial(kernel, along, across), out_shape=pltpu....  24.7 us
    unnamed x1, local copies, waits for them, and re-layouts  0.63 us

profile of v6, /device:TPU:1, one launch (start us, length us, event | category | flops | bytes accessed | tf_op | source)
XLA Modules:
  0.0 25.3 jit_solution(5050914706703263881)
XLA Ops:
  0.0 24.7 %shard_map.46 = bf16[128,256]{1,0:T(8,128)(2,1)S(1)} custom-call(s32[1,64]{1,0:T(1,128)} %c_ref.1, bf16[128,256]{1,0:T(8,128)(2,1)} %f_ref.1, bf16[1,64,128,128]{3,2,1,0:T(8,128)(2,1)} %t_ref.1, bf16[256,256]{1,0:T(8,128)(2,1)} %w_ref.1), custom_call_target="tpu_custom_call" | custom-call | flops 536870912 | bytes 4194304 | tf_op jit(solution)/shard_map/pallas_call | solution.py:228
  24.7 0.6 %copy.6 = bf16[128,256]{1,0:T(8,128)(2,1)} copy(bf16[128,256]{1,0:T(8,128)(2,1)S(1)} %shard_map.46) | data formatting | bytes 131072

commit v7 on v6

--- a/solution.py
+++ b/solution.py
@@ -207,7 +207,7 @@
         right = jnp.concatenate([blocks[col_ref[0, i * group + g]] for g in range(group)], axis=0)
         return total + jnp.dot(left, right, preferred_element_type=jnp.float32)
 
-    total = lax.fori_loop(0, number // group, step, jnp.zeros(out_ref.shape, jnp.float32))
+    total = lax.fori_loop(0, number // group, step, jnp.zeros(out_ref.shape, jnp.float32), unroll=True)
     aggregated = total.astype(jnp.bfloat16)
     product = jnp.dot(aggregated, weight[...], preferred_element_type=jnp.float32)
     out_ref[...] = jnp.maximum(product, 0.0).astype(out_ref.dtype)

time: 25.5 us -> 24.2 us (0.949)
  Pallas kernels: 24.7 us -> 23.4 us
    pallas_call x1, Pallas kernels: 24.7 us -> 23.4 us  [on_device(): pl.pallas_call(functools.partial(kernel, along, across), out_shape=pltpu....]
where the time goes in v7:
time: 24.2 us; the launch traced here: 24.1 us
  Pallas kernels  23.4 us (97%)
  local copies, waits for them, and re-layouts  0.63 us (3%)
    pallas_call x1, Pallas kernels, on_device(): pl.pallas_call(functools.partial(kernel, along, across), out_shape=pltpu....  23.4 us
    unnamed x1, local copies, waits for them, and re-layouts  0.63 us

profile of v7, /device:TPU:1, one launch (start us, length us, event | category | flops | bytes accessed | tf_op | source)
XLA Modules:
  0.0 24.1 jit_solution(11083803875789255527)
XLA Ops:
  0.0 23.4 %shard_map.46 = bf16[128,256]{1,0:T(8,128)(2,1)S(1)} custom-call(s32[1,64]{1,0:T(1,128)} %c_ref.1, bf16[128,256]{1,0:T(8,128)(2,1)} %f_ref.1, bf16[1,64,128,128]{3,2,1,0:T(8,128)(2,1)} %t_ref.1, bf16[256,256]{1,0:T(8,128)(2,1)} %w_ref.1), custom_call_target="tpu_custom_call" | custom-call | flops 536870912 | bytes 4194304 | tf_op jit(solution)/shard_map/pallas_call | solution.py:228
  23.5 0.6 %copy.6 = bf16[128,256]{1,0:T(8,128)(2,1)} copy(bf16[128,256]{1,0:T(8,128)(2,1)S(1)} %shard_map.46) | data formatting | bytes 131072

commit v8 on v7

--- a/solution.py
+++ b/solution.py
@@ -20,16 +20,13 @@
         if item[1]:
             keys.append(("column", item))
         keys.append(("beside", item))
-        keys.append(("sibling", item, 0, 0))
-        keys.append(("sibling", item, 1, 0))
         for q in range(1, across):
             keys.append(("across", item, q))
             keys.extend(("diagonal", item, q, h) for h in range(3))
-            keys.append(("sibling", item, 0, q))
-            keys.extend(("sibling diagonal", item, q, h) for h in range(3))
     return {key: spot for spot, key in enumerate(keys)}
 
-def kernel(columns, across, c_ref, f_ref, t_ref, w_ref, out_ref, blocks, tiles, weight, col_ref, send_sems, recv_sems, local_sems):
+
+def kernel(columns, across, c_ref, f_ref, t_ref, w_ref, out_ref, blocks, tiles, weight, col_ref, send_sems, recv_sems, all_sent, all_came, local_sems):
     rep = 2 * across
     side_rows = blocks.shape[1]
     half = side_rows // 2
@@ -38,7 +35,7 @@
     a, b = section_at // 2, section_at % 2
     x, c = rep_at // 2, rep_at % 2
     spots = arrivals(columns, across)
-    sent, climbed = [], []
+    climbed = []
 
     def device(item, beside, q, other):
         at = lax.rem(x + q, across) if q else x
@@ -73,13 +70,12 @@
         else:
             pl.when(condition)(work)
 
-    def send(src, dst, to, key, condition):
+    def send(src, dst, to, key):
         copy = pltpu.make_async_remote_copy(
-            src_ref=src, dst_ref=dst, send_sem=send_sems.at[spots[key]], recv_sem=recv_sems.at[spots[key]],
+            src_ref=src, dst_ref=dst, send_sem=send_sems.at[spots[key]] if key[0] == "column" else all_sent,
+            recv_sem=all_came if key[0] == "sibling" else recv_sems.at[spots[key]],
             device_id=to, device_id_type=pl.DeviceIdType.MESH)
         copy.start()
-        if condition is not None:
-            sent.append((src.shape[0], key, condition))
 
     def arrive(dst, key):
         pltpu.make_async_remote_copy(
@@ -110,7 +106,7 @@
     def climb(s):
         for side, condition in ((-1, a + s < columns), (1, a >= s)):
             to, key = device((-side, s), 0, 0, 0), ("column", (side, s))
-            only(condition, functools.partial(send, f_ref, block(here, 0, 0), to, key, None))
+            only(condition, functools.partial(send, f_ref, block(here, 0, 0), to, key))
             climbed.append((s, key, condition))
 
     def wait_climb(s):
@@ -121,17 +117,17 @@
     def pass_on(src, item):
         on = a + 1 < columns if item[0] < 0 else a >= 1
         to, key = device((-item[0], 1), 0, 0, 0), ("column", (item[0], 2))
-        only(on, lambda: send(src, src, to, key, None))
+        only(on, lambda: send(src, src, to, key))
 
     def spread(src, item):
         dst = block(item, 0, 0)
         for q in range(1, across):
-            send(src, dst, device(here, 0, q, 0), ("across", item, q), lambda: there(item))
-        send(src, dst, beside, ("beside", item), lambda: there(item))
+            send(src, dst, device(here, 0, q, 0), ("across", item, q))
+        send(src, dst, beside, ("beside", item))
         if direct(item):
             for q in range(1, across):
-                send(src, dst, device(here, 1, q, 0), ("diagonal", item, q, 0), lambda: there(item))
-        send(src, dst, sibling, ("sibling", item, 0, 0), lambda: there(item))
+                send(src, dst, device(here, 1, q, 0), ("diagonal", item, q, 0))
+        send(src, dst, sibling, ("sibling",))
 
     def receive(item):
         got = block(item, 0, 0)
@@ -145,29 +141,21 @@
             got = block(item, 0, across - q)
             arrive(got, ("across", item, q))
             if not direct(item):
-                send(part(got, 1), part(got, 1), beside, ("diagonal", item, q, 1), lambda: there(item))
-            send(got, got, sibling, ("sibling", item, 0, q), lambda: there(item))
+                send(part(got, 1), part(got, 1), beside, ("diagonal", item, q, 1))
+            send(got, got, sibling, ("sibling",))
         got = block(item, 1, 0)
         arrive(got, ("beside", item))
         for q in range(1, across):
             if not direct(item):
-                send(part(got, 2), part(got, 2), device(here, 0, q, 0), ("diagonal", item, q, 2), lambda: there(item))
-        send(got, got, sibling, ("sibling", item, 1, 0), lambda: there(item))
+                send(part(got, 2), part(got, 2), device(here, 0, q, 0), ("diagonal", item, q, 2))
+        send(got, got, sibling, ("sibling",))
 
     def diagonal(item):
         for q in range(1, across):
             for h in pieces(item):
                 got = part(block(item, 1, across - q), h)
                 arrive(got, ("diagonal", item, q, h))
-                send(got, got, sibling, ("sibling diagonal", item, q, h), lambda: there(item))
-
-    def from_sibling(item):
-        arrive(block(item, 0, 0, 1), ("sibling", item, 0, 0))
-        arrive(block(item, 1, 0, 1), ("sibling", item, 1, 0))
-        for q in range(1, across):
-            arrive(block(item, 0, across - q, 1), ("sibling", item, 0, q))
-            for h in pieces(item):
-                arrive(part(block(item, 1, across - q, 1), h), ("sibling diagonal", item, q, h))
+                send(got, got, sibling, ("sibling",))
 
     if columns > 1:
         climb(1)
@@ -191,9 +179,10 @@
             if 0 <= at < len(rounds) and not (stage is receive and at == 0):
                 for item in rounds[at]:
                     only(there(item), functools.partial(stage, item))
-    for items in rounds:
-        for item in items:
-            only(there(item), functools.partial(from_sibling, item))
+    whole = blocks.at[pl.ds(0, columns * 2 * across)]
+    pltpu.make_async_remote_copy(
+        src_ref=whole, dst_ref=whole, send_sem=all_sent, recv_sem=all_came,
+        device_id=sibling, device_id_type=pl.DeviceIdType.MESH).wait_recv()
     own.wait()
     load_columns.wait()
     load_tiles.wait()
@@ -217,8 +206,10 @@
     if columns > 2:
         for item, condition in (((-1, 2), (a >= 1) & (a + 1 < columns)), ((1, 2), (a >= 1) & (a + 1 < columns))):
             only(condition, functools.partial(gone, f_ref.shape[0], ("column", item)))
-    for rows, key, condition in sent:
-        only(condition(), functools.partial(gone, rows, key))
+    whole = blocks.at[pl.ds(0, columns * (4 * across - 1))]
+    pltpu.make_async_remote_copy(
+        src_ref=whole, dst_ref=whole, send_sem=all_sent, recv_sem=all_came,
+        device_id=sibling, device_id_type=pl.DeviceIdType.MESH).wait_send()
 
 
 def on_device(sections, reps, features, tiles, columns, weight):
@@ -237,6 +228,8 @@
             pltpu.SMEM(columns.shape, columns.dtype),
             pltpu.SemaphoreType.DMA((arriving,)),
             pltpu.SemaphoreType.DMA((arriving,)),
+            pltpu.SemaphoreType.DMA,
+            pltpu.SemaphoreType.DMA,
             pltpu.SemaphoreType.DMA((4,)),
         ],
         compiler_params=pltpu.CompilerParams(

time: 24.2 us -> 23.4 us (0.967)
  Pallas kernels: 23.4 us -> 22.7 us
    pallas_call x1, Pallas kernels: 23.4 us -> 22.7 us  [on_device(): pl.pallas_call(functools.partial(kernel, along, across), out_shape=pltpu....]
where the time goes in v8:
time: 23.4 us; the launch traced here: 23.3 us
  Pallas kernels  22.7 us (97%)
  local copies, waits for them, and re-layouts  0.63 us (3%)
    pallas_call x1, Pallas kernels, on_device(): pl.pallas_call(functools.partial(kernel, along, across), out_shape=pltpu....  22.7 us
    unnamed x1, local copies, waits for them, and re-layouts  0.63 us

profile of v8, /device:TPU:1, one launch (start us, length us, event | category | flops | bytes accessed | tf_op | source)
XLA Modules:
  0.0 23.3 jit_solution(14045168388584511387)
XLA Ops:
  0.0 22.7 %shard_map.46 = bf16[128,256]{1,0:T(8,128)(2,1)S(1)} custom-call(s32[1,64]{1,0:T(1,128)} %c_ref.1, bf16[128,256]{1,0:T(8,128)(2,1)} %f_ref.1, bf16[1,64,128,128]{3,2,1,0:T(8,128)(2,1)} %t_ref.1, bf16[256,256]{1,0:T(8,128)(2,1)} %w_ref.1), custom_call_target="tpu_custom_call" | custom-call | flops 536870912 | bytes 4194304 | tf_op jit(solution)/shard_map/pallas_call | solution.py:219
  22.7 0.6 %copy.6 = bf16[128,256]{1,0:T(8,128)(2,1)} copy(bf16[128,256]{1,0:T(8,128)(2,1)S(1)} %shard_map.46) | data formatting | bytes 131072

commit v9 on v8

--- a/solution.py
+++ b/solution.py
@@ -6,7 +6,7 @@
 from jax.experimental.pallas import tpu as pltpu
 from jax.sharding import PartitionSpec as P
 
-GROUP = 8
+GROUP = 2
 
 def flip(index, wanted):
     return index + wanted - 2 * wanted * (index % 2)

time: 23.4 us -> 23.4 us (level)
  no operation moved by 1% of the time
where the time goes in v9:
time: 23.4 us; the launch traced here: 23.3 us
  Pallas kernels  22.7 us (97%)
  local copies, waits for them, and re-layouts  0.63 us (3%)
    pallas_call x1, Pallas kernels, on_device(): pl.pallas_call(functools.partial(kernel, along, across), out_shape=pltpu....  22.7 us
    unnamed x1, local copies, waits for them, and re-layouts  0.63 us

profile of v9, /device:TPU:1, one launch (start us, length us, event | category | flops | bytes accessed | tf_op | source)
XLA Modules:
  0.0 23.3 jit_solution(12913591562842087972)
XLA Ops:
  0.0 22.7 %shard_map.46 = bf16[128,256]{1,0:T(8,128)(2,1)S(1)} custom-call(s32[1,64]{1,0:T(1,128)} %c_ref.1, bf16[128,256]{1,0:T(8,128)(2,1)} %f_ref.1, bf16[1,64,128,128]{3,2,1,0:T(8,128)(2,1)} %t_ref.1, bf16[256,256]{1,0:T(8,128)(2,1)} %w_ref.1), custom_call_target="tpu_custom_call" | custom-call | flops 536870912 | bytes 4194304 | tf_op jit(solution)/shard_map/pallas_call | solution.py:219
  22.7 0.6 %copy.6 = bf16[128,256]{1,0:T(8,128)(2,1)} copy(bf16[128,256]{1,0:T(8,128)(2,1)S(1)} %shard_map.46) | data formatting | bytes 131072

commit v10 on v8

--- a/solution.py
+++ b/solution.py
@@ -48,7 +48,7 @@
         return blocks.at[s * rep + r]
 
     def direct(item):
-        return item[1] > 1 and item[1] == columns - 1
+        return item[1] != 1
 
     def pieces(item):
         return (0,) if direct(item) else (1, 2)

time: 23.4 us -> 23.8 us (1.017)
  Pallas kernels: 22.7 us -> 23 us
    pallas_call x1, Pallas kernels: 22.7 us -> 23 us  [on_device(): pl.pallas_call(functools.partial(kernel, along, across), out_shape=pltpu....]
where the time goes in v10:
time: 23.8 us; the launch traced here: 23.6 us
  Pallas kernels  23 us (97%)
  local copies, waits for them, and re-layouts  0.63 us (3%)
    pallas_call x1, Pallas kernels, on_device(): pl.pallas_call(functools.partial(kernel, along, across), out_shape=pltpu....  23 us
    unnamed x1, local copies, waits for them, and re-layouts  0.63 us

profile of v10, /device:TPU:1, one launch (start us, length us, event | category | flops | bytes accessed | tf_op | source)
XLA Modules:
  0.0 23.6 jit_solution(3742570795591845099)
XLA Ops:
  0.0 23.0 %shard_map.46 = bf16[128,256]{1,0:T(8,128)(2,1)S(1)} custom-call(s32[1,64]{1,0:T(1,128)} %c_ref.1, bf16[128,256]{1,0:T(8,128)(2,1)} %f_ref.1, bf16[1,64,128,128]{3,2,1,0:T(8,128)(2,1)} %t_ref.1, bf16[256,256]{1,0:T(8,128)(2,1)} %w_ref.1), custom_call_target="tpu_custom_call" | custom-call | flops 536870912 | bytes 4194304 | tf_op jit(solution)/shard_map/pallas_call | solution.py:219
  23.0 0.6 %copy.6 = bf16[128,256]{1,0:T(8,128)(2,1)} copy(bf16[128,256]{1,0:T(8,128)(2,1)S(1)} %shard_map.46) | data formatting | bytes 131072
